TPU v7x, 512 devices: a whole 4x8x8 slice. The times are simulated.
512 devices in a mesh: pair: 32 (over z_lo, y, core), va: 4 (over z_hi), vb: 4 (over x).
Axes of the slice: x: 4, y: 8, z: 8 (z_hi: 4, z_lo: 2; z = z_hi * 2 + z_lo), core: 2. Of those that a mesh axis runs over, the one named last changes fastest.
Arguments:
- driver: float32 [1600, 256, 256], P('pair', 'va', 'vb'), may hold values from -6 to 6
- coupling: float32 [1600, 1600], P('vb'), may hold values from -0.15625 to 0.15625
- eps_occ: float32 [40], replicated, may hold values from -2 to -0.5
- eps_vir: float32 [256], replicated, may hold values from 0.3 to 3
Outputs:
- spin_adapted: float32 [1600, 256, 256], P('vb', ('va', 'pair'))
All inputs are finite; a program needn't handle non-finite values.
Results may differ from a plain program's by a relative error of at most 0.0001.
Values sent between devices are 32-bit elements; how exact they have to be, the bound alone decides.
A program may use at most 64 MiB of HBM per device.

v0:
```python
import jax
import jax.numpy as jnp
from jax import lax
from jax.sharding import PartitionSpec as P

ITERS = 2


def apply_ladder(matrix, right):
    return jnp.dot(
        matrix, right, precision=lax.Precision.HIGHEST, preferred_element_type=jnp.float32
    )


def to_elements(values):
    return lax.all_to_all(
        lax.all_to_all(values, "pair", split_axis=1, concat_axis=0, tiled=True),
        "vb",
        split_axis=0,
        concat_axis=1,
        tiled=True,
    )


def on_device(driver, coupling, eps_occ, eps_vir):
    npair = lax.axis_size("pair")
    nva = lax.axis_size("va")
    nvb = lax.axis_size("vb")
    pidx = lax.axis_index("pair")
    aidx = lax.axis_index("va")
    bidx = lax.axis_index("vb")
    pblock, tile_a, tile_b = driver.shape
    pairs = pblock * npair
    nvirt = tile_a * nva
    rchunk = tile_a // npair
    iblock = pairs // nvb
    pair_energy = (eps_occ[:, None] + eps_occ[None, :]).reshape(pairs)
    pair_part = lax.dynamic_slice_in_dim(pair_energy, pidx * pblock, pblock)
    row_tile = lax.dynamic_slice_in_dim(eps_vir, aidx * tile_a, tile_a)
    col_tile = lax.dynamic_slice_in_dim(eps_vir, bidx * tile_b, tile_b)
    virtual_sum = row_tile[:, None] + col_tile[None, :]
    denom_pair = (virtual_sum[None] - pair_part[:, None, None]).reshape(pblock, tile_a * tile_b)
    driver_flat = driver.reshape(pblock, tile_a * tile_b)
    state = driver_flat / denom_pair
    for step in range(ITERS):
        moved = lax.all_to_all(state, "pair", split_axis=1, concat_axis=0, tiled=True)
        product = apply_ladder(coupling, lax.all_gather(moved, "vb", axis=1, tiled=True))
        widened = lax.all_to_all(product, "vb", split_axis=1, concat_axis=0, tiled=True)
        image = lax.all_to_all(widened, "pair", split_axis=0, concat_axis=1, tiled=True)
        state = (image + driver_flat) / denom_pair
    final = to_elements(state)
    t_rows = (
        final.reshape(iblock, nvb, rchunk, tile_b)
        .transpose(0, 2, 1, 3)
        .reshape(iblock, rchunk, nvirt)
    )
    outgoing = (
        t_rows.reshape(iblock, rchunk, nva, npair, rchunk)
        .transpose(0, 3, 2, 4, 1)
        .reshape(iblock, nvirt * rchunk)
    )
    received = lax.all_to_all(outgoing, ("pair", "va"), split_axis=1, concat_axis=1, tiled=True)
    mirrored = (
        received.reshape(iblock, npair, nva, rchunk, rchunk)
        .transpose(0, 3, 2, 1, 4)
        .reshape(iblock, rchunk, nvirt)
    )
    return 2.0 * t_rows - mirrored


def solution(mesh):
    return jax.shard_map(
        on_device,
        mesh=mesh,
        in_specs=(P("pair", "va", "vb"), P("vb", None), P(), P()),
        out_specs=P("vb", ("va", "pair"), None),
        check_vma=False,
    )
```

profile of v0, /device:TPU:1, one launch (start us, length us, event | category | flops | bytes accessed | tf_op | source)
XLA Modules:
  0.0 408.5 jit_solution(8710010117565487323)
XLA Ops:
  8.6 1.7 reshape.113
  11.1 34.2 %all_to_all.134 = f32[50,32,128]{2,0,1:T(8,128)} all-to-all(f32[50,32,128]{2,0,1:T(8,128)S(1)} %copy.44), channel_id=1, replica_groups=mesh['pair'=32,'va'=4,'vb'=4] {'pair'}, dimensions={1} | all-to-all | bytes 1638400 | tf_op jit(solution)/shard_map/all_to_all | solution.py:46
  45.3 2.1 all_to_all.102
  47.5 50.6 %all-gather.3.cloned.1.call-done = f32[1600,512]{1,0:T(8,128)} async-done(((f32[1600,128]{1,0:T(8,128)}), f32[1600,512]{1,0:T(8,128)}) %all-gather.3.cloned.1.call-update) | async-done | bytes 3276816 | tf_op jit(solution)/shard_map/all_gather | solution.py:47
  98.1 6.7 %convolution_bitcast_fusion.1 = f32[50,4,8,128]{3,2,1,0:T(8,128)S(1)} fusion(f32[1600,512]{1,0:T(8,128)} %all-gather.3.cloned.1.call-done, f32[400,1600]{1,0:T(8,128)S(1)} %copy-done), kind=kOutput, calls=%fused_computation.4 | convolution fusion | flops 3932160000 | bytes 6656000 | tf_op jit(solution)/shard_map/dot_general | solution.py:10
  104.9 14.4 %all_to_all.135 = f32[400,4,128]{2,0,1:T(8,128)} all-to-all(f32[400,4,128]{2,0,1:T(8,128)S(1)} %bitcast.57), channel_id=1, replica_groups=mesh['pair'=32,'va'=4,'vb'=4] {'vb'}, dimensions={1} | all-to-all | bytes 1638400 | tf_op jit(solution)/shard_map/all_to_all | solution.py:48
  119.3 2.1 all_to_all.106
  121.5 34.5 %all_to_all.136 = f32[32,50,128]{2,1,0:T(8,128)S(1)} all-to-all(f32[32,50,128]{2,1,0:T(8,128)} %all_to_all.106), channel_id=1, replica_groups=mesh['pair'=32,'va'=4,'vb'=4] {'pair'}, dimensions={0} | all-to-all | bytes 1638400 | tf_op jit(solution)/shard_map/all_to_all | solution.py:49
  156.7 29.5 %all_to_all.137 = f32[50,32,128]{2,0,1:T(8,128)} all-to-all(f32[50,32,128]{2,0,1:T(8,128)S(1)} %copy.47), channel_id=1, replica_groups=mesh['pair'=32,'va'=4,'vb'=4] {'pair'}, dimensions={1} | all-to-all | bytes 1638400 | tf_op jit(solution)/shard_map/all_to_all | solution.py:46
  186.2 2.1 all_to_all.111
  188.4 45.9 %all-gather.5.cloned.1.call-done = f32[1600,512]{1,0:T(8,128)} async-done(((f32[1600,128]{1,0:T(8,128)}), f32[1600,512]{1,0:T(8,128)}) %all-gather.5.cloned.1.call-update) | async-done | bytes 3276816 | tf_op jit(solution)/shard_map/all_gather | solution.py:47
  234.2 6.7 %convolution_bitcast_fusion = f32[50,4,8,128]{3,2,1,0:T(8,128)S(1)} fusion(f32[1600,512]{1,0:T(8,128)} %all-gather.5.cloned.1.call-done, f32[400,1600]{1,0:T(8,128)S(1)} %copy-done), kind=kOutput, calls=%fused_computation.3 | convolution fusion | flops 3932160000 | bytes 6656000 | tf_op jit(solution)/shard_map/dot_general | solution.py:10
  241.0 14.5 %all_to_all.138 = f32[400,4,128]{2,0,1:T(8,128)} all-to-all(f32[400,4,128]{2,0,1:T(8,128)S(1)} %bitcast.58), channel_id=1, replica_groups=mesh['pair'=32,'va'=4,'vb'=4] {'vb'}, dimensions={1} | all-to-all | bytes 1638400 | tf_op jit(solution)/shard_map/all_to_all | solution.py:48
  255.5 2.1 all_to_all.115
  257.6 34.4 %all_to_all.139 = f32[32,50,128]{2,1,0:T(8,128)S(1)} all-to-all(f32[32,50,128]{2,1,0:T(8,128)} %all_to_all.115), channel_id=1, replica_groups=mesh['pair'=32,'va'=4,'vb'=4] {'pair'}, dimensions={0} | all-to-all | bytes 1638400 | tf_op jit(solution)/shard_map/all_to_all | solution.py:49
  292.8 29.5 %all_to_all.140 = f32[50,32,128]{2,0,1:T(8,128)} all-to-all(f32[50,32,128]{2,0,1:T(8,128)S(1)} %copy.50), channel_id=1, replica_groups=mesh['pair'=32,'va'=4,'vb'=4] {'pair'}, dimensions={1} | all-to-all | bytes 1638400 | tf_op jit(solution)/shard_map/all_to_all | solution.py:17
  322.4 2.1 all_to_all.120
  324.5 13.7 %all_to_all.141 = f32[4,400,128]{2,1,0:T(8,128)S(1)} all-to-all(f32[4,400,128]{2,1,0:T(8,128)} %all_to_all.120), channel_id=1, replica_groups=mesh['pair'=32,'va'=4,'vb'=4] {'vb'}, dimensions={0} | all-to-all | bytes 1638400 | tf_op jit(solution)/shard_map/all_to_all | solution.py:16
  338.1 1.3 copy.51
  339.5 1.9 copy.53
  341.4 1.8 copy.61
  343.1 3.2 reshape.117
  346.3 14.6 %all-to-all-start.8 = ((f32[400,128,4]{0,2,1:T(4,128)}), f32[400,128,4]{0,2,1:T(4,128)}, u32[]{:S(2)}, u32[]{:S(2)}) async-start(f32[400,128,4]{0,2,1:T(4,128)} %reshape.117), calls=%async_computation.8 | async-start | bytes 2097152 | tf_op jit(solution)/shard_map/all_to_all | solution.py:62
  361.0 1.4 broadcast_multiply_fusion
  363.4 1.5 copy.58
  364.9 25.1 %all-to-all-done.8 = f32[400,128,4]{0,2,1:T(4,128)} async-done(((f32[400,128,4]{0,2,1:T(4,128)}), f32[400,128,4]{0,2,1:T(4,128)}, u32[]{:S(2)}, u32[]{:S(2)}) %all-to-all-start.8) | async-done | bytes 819232 | tf_op jit(solution)/shard_map/all_to_all | solution.py:62
  390.0 3.2 reshape.118
  393.1 1.6 copy.71
  394.8 1.8 copy.57
  396.5 2.2 copy.59
  398.7 1.3 sub.23
  400.1 1.5 copy.60
  (24 shorter events, 5.5 us)
Async XLA Ops:
  6.5 91.6 %copy-start = (f32[400,1600]{1,0:T(8,128)S(1)}, f32[400,1600]{1,0:T(8,128)}, u32[]{:S(2)}) copy-start(f32[400,1600]{1,0:T(8,128)} %param.5) | copy-start | bytes 7680004
  6.5 91.5 %all-gather.3.cloned.1.call-start = ((), (), s32[]{:S(2)}) async-start(), calls=%async_computation.9 | async-start | bytes 4096000 | tf_op jit(solution)/shard_map/all_gather | solution.py:47
  47.5 186.8 %all-gather.5.cloned.1.call-start = ((), (), s32[]{:S(2)}) async-start(), calls=%async_computation.10 | async-start | bytes 4096000 | tf_op jit(solution)/shard_map/all_gather | solution.py:47
  346.3 43.6 %all-to-all-start.8 = ((f32[400,128,4]{0,2,1:T(4,128)}), f32[400,128,4]{0,2,1:T(4,128)}, u32[]{:S(2)}, u32[]{:S(2)}) async-start(f32[400,128,4]{0,2,1:T(4,128)} %reshape.117), calls=%async_computation.8 | async-start | bytes 2097152 | tf_op jit(solution)/shard_map/all_to_all | solution.py:62
Sparse Core Ops, SparseCore 0:
  47.6 50.4 all-gather.2
  188.5 45.7 all-gather.4
where the time goes:
time: 411 us; the launch traced here: 408 us
  blocking collectives  205 us (50%)
  waiting for transfers between devices  122 us (30%)
  local copies, waits for them, and re-layouts  36.3 us (9%)
  starting transfers between devices  14.7 us (4%)
  between operations  13.5 us (3%)
  matrix products  13.4 us (3%)
  other arithmetic  4.21 us (1%)
    all_gather x2, waiting for transfers between devices, on_device(): lax.all_gather(moved, 'vb', axis=1, tiled=True)  96.5 us
    all_to_all x2, blocking collectives, on_device(): lax.all_to_all(widened, 'pair', split_axis=0, concat_axis=1, tiled=True)  68.9 us
    all_to_all x2, blocking collectives, on_device(): lax.all_to_all(state, 'pair', split_axis=1, concat_axis=0, tiled=True)  63.7 us
    all_to_all x1, blocking collectives, to_elements(): lax.all_to_all(values, 'pair', split_axis=1, concat_axis=0, tiled=True)  29.5 us
    all_to_all x2, blocking collectives, on_device(): lax.all_to_all(product, 'vb', split_axis=1, concat_axis=0, tiled=True)  28.9 us
    all_to_all x1, waiting for transfers between devices, on_device(): lax.all_to_all(outgoing, ('pair', 'va'), split_axis=1, concat_axis=1, til...  25.1 us
    all_to_all x1, starting transfers between devices, on_device(): lax.all_to_all(outgoing, ('pair', 'va'), split_axis=1, concat_axis=1, til...  14.6 us
    all_to_all x1, blocking collectives, to_elements(): lax.all_to_all(lax.all_to_all(values, 'pair', split_axis=1, concat_axis=0...  13.7 us
  transfers between devices with their start and end apart: 3, of which 3 were waited for; matrix products, arithmetic and copies ran while one was open for 1% of the time, Pallas kernels for 0%

commit v1 on v0

v1 whole, which is shorter than its diff:
```python
import jax
import jax.numpy as jnp
from jax import lax
from jax.experimental import pallas as pl
from jax.experimental.pallas import tpu as pltpu
from jax.sharding import PartitionSpec as P

MESH = pl.DeviceIdType.MESH
F32 = jnp.float32
BF16 = jnp.bfloat16

PAIRS = 1600
NOCC = 40
BLK = 400
SRC = 50
ZROWS = (16, 8)
ZOFF = (0, 128)
XROWS = (72, 136)
XOFF = (192, 264)
XHALF = (40, 72)


def kernel(
    drv, cpl, eo, evs, evv, out,
    din, snd, rcv, wf, whi, wlo, dcol, rden, rhs, occ, t2, r1, tn, msend, mrecv, up, qs,
    lsem, vsem, wxs, wxr, xs, xr, zs, zr, cs, cr, ds, dr, c1s, c1r, ms, mr, us, ur,
):
    p = lax.axis_index("pair")
    za = lax.axis_index("va")
    x = lax.axis_index("vb")
    h = lax.rem(p, 2)
    k = p // 2
    y = lax.rem(k, 8)
    zl = k // 8
    z = 2 * za + zl

    def at(pp, aa, xx):
        return {"pair": pp, "va": aa, "vb": xx}

    def zdev(step):
        zz = lax.rem(z + step + 8, 8)
        return at(lax.rem(zz, 2) * 16 + y * 2 + h, zz // 2, x)

    def rcopy(src, dst, s, r, dev):
        return pltpu.make_async_remote_copy(
            src_ref=src, dst_ref=dst, send_sem=s, recv_sem=r, device_id=dev, device_id_type=MESH
        )

    other = at(p + 1 - 2 * h, za, x)

    wcopy = pltpu.make_async_copy(cpl, wf.at[0], lsem.at[0])
    wcopy.start()
    dcopy = pltpu.make_async_copy(drv, din, lsem.at[1])
    dcopy.start()

    bar = pltpu.get_barrier_semaphore()

    @pl.loop(1, 32)
    def _(i):
        pl.semaphore_signal(bar, inc=1, device_id=at(lax.rem(p + i, 32), za, x), device_id_type=MESH)

    for i in range(1, 4):
        pl.semaphore_signal(bar, inc=1, device_id=at(p, za, lax.rem(x + i, 4)), device_id_type=MESH)
        pl.semaphore_signal(bar, inc=1, device_id=at(p, lax.rem(za + i, 4), x), device_id_type=MESH)
    pl.semaphore_signal(bar, inc=1, device_id=zdev(2 * zl - 1), device_id_type=MESH)

    for j in range(NOCC):
        occ[pl.ds(j, 1), :] = jnp.full((1, 128), eo[j], F32)
    lane = lax.broadcasted_iota(jnp.int32, (8, 128), 1)
    cols = jnp.broadcast_to(jnp.where(x >= 2, evv[1:2, :], evv[0:1, :]), (8, 128))
    off = 64 * lax.rem(x, 2) + 32 * h
    cols = pltpu.roll(cols, lax.rem(128 - off, 128), 1)
    vsum = jnp.zeros((8, 128), F32)
    for a in range(4):
        here = (cols if a == 0 else pltpu.roll(cols, 32 * a, 1)) + evs[64 * za + 4 * k + a]
        vsum = jnp.where(lane // 32 == a, here, vsum)
    vrow = vsum[0:1, :]

    @pl.loop(0, NOCC)
    def _(i):
        den = vrow - (occ[...] + eo[i])
        rden[pl.ds(pl.multiple_of(40 * i, 8), 40), :] = 1.0 / den

    wcopy.wait()
    dcopy.wait()
    pl.semaphore_wait(bar, 38)
    for i in range(1, 4):
        pl.semaphore_signal(vsem, inc=1, device_id=at(p, lax.rem(za + i, 4), x), device_id_type=MESH)

    def zslice(hh, zz):
        return pl.ds(pl.multiple_of(ZOFF[hh] + ZROWS[hh] * zz, 8), ZROWS[hh])

    def xslice(hh, half):
        if half is None:
            return pl.ds(XOFF[hh], XROWS[hh])
        return pl.ds(XOFF[hh], XHALF[hh]) if half == 0 else pl.ds(XOFF[hh] + XHALF[hh], XROWS[hh] - XHALF[hh])

    def wx(hh, i):
        return rcopy(
            wf.at[0, zslice(hh, z), :], wf.at[4 - i, zslice(hh, z), :], wxs.at[i - 1], wxr.at[3 - i],
            at(p, za, lax.rem(x + i, 4)),
        )

    def xcopy(hh, n):
        right, left = at(p, za, lax.rem(x + 1, 4)), at(p, za, lax.rem(x + 3, 4))
        if n == 0:
            src, dst, dev = wf.at[0, xslice(hh, None), :], wf.at[3, xslice(hh, None), :], right
        elif n == 1:
            src, dst, dev = wf.at[0, xslice(hh, None), :], wf.at[1, xslice(hh, None), :], left
        elif n == 2:
            src, dst, dev = wf.at[3, xslice(hh, 0), :], wf.at[2, xslice(hh, 0), :], right
        else:
            src, dst, dev = wf.at[1, xslice(hh, 1), :], wf.at[2, xslice(hh, 1), :], left
        return rcopy(src, dst, xs.at[n], xr.at[n], dev)

    def xswap(hh, n):
        rel, half = ((3, None), (1, None), (2, 0), (2, 1))[n]
        ref = wf.at[rel, xslice(hh, half), :]
        return rcopy(ref, ref, cs.at[8 + n], cr.at[8 + n], other)

    def zcopy(hh, up, d):
        src = wf.at[pl.ds(1, 3), zslice(hh, lax.rem(z + 8 + (-d if up else d), 8)), :]
        n = d if up else 4 + d
        return rcopy(src, src, zs.at[n], zr.at[n], zdev(1 if up else -1))

    def zwait(hh, up, d):
        dst = wf.at[pl.ds(1, 3), zslice(hh, lax.rem(z + 8 + (-d if up else d), 8)), :]
        n = d - 1 if up else 4 + d - 1
        return rcopy(dst, dst, zs.at[n], zr.at[n], zdev(1 if up else -1))

    def zswap(hh, dz):
        ref = wf.at[pl.ds(1, 3), zslice(hh, lax.rem(z + dz, 8)), :]
        return rcopy(ref, ref, cs.at[dz], cr.at[dz], other)

    ups, downs = (4, 3), (3, 4)

    for hh in range(2):
        @pl.when(h == hh)
        def _():
            for i in (2, 1, 3):
                wx(hh, i).start()
            for n in range(2):
                xcopy(hh, n).start()

    def dcp(i, d, src):
        return rcopy(snd.at[d], rcv.at[src], ds.at[i], dr.at[src], at(d, za, x))

    @pl.loop(0, 16)
    def _(i):
        kk = lax.rem(k + i, 16)
        rows = [din[pl.ds(4 * kk + a, SRC, stride=64), :] for a in range(4)]
        for hh in range(2):
            d = 2 * kk + hh
            snd[d] = jnp.concatenate([r[:, 32 * hh : 32 * hh + 32] for r in rows], axis=1)

            @pl.when(d != p)
            def _():
                dcp(2 * i + hh, d, p).start()

    def conv(rel):
        @pl.loop(0, 5)
        def _(i):
            rows = pl.ds(pl.multiple_of(80 * i, 16), 80)
            v = wf[rel, rows, :]
            hi = v.astype(BF16)
            whi[rel, rows, :] = hi
            wlo[rel, rows, :] = (v - hi.astype(F32)).astype(BF16)

    def ring(d):
        for hh in range(2):
            @pl.when(h == hh)
            def _():
                if d == 0:
                    for i in range(1, 4):
                        wx(hh, i).wait_recv()
                    zcopy(hh, True, 0).start()
                    zcopy(hh, False, 0).start()
                    zswap(hh, 0).start()
                else:
                    if d <= ups[hh]:
                        zwait(hh, True, d).wait_recv()
                        if d < ups[hh]:
                            zcopy(hh, True, d).start()
                        zswap(hh, 8 - d).start()
                    if d <= downs[hh]:
                        zwait(hh, False, d).wait_recv()
                        if d < downs[hh]:
                            zcopy(hh, False, d).start()
                        zswap(hh, d).start()

    ring(0)
    conv(0)
    ring(1)
    ring(2)
    for hh in range(2):
        @pl.when(h == hh)
        def _():
            for n in range(2):
                xcopy(hh, n).wait_recv()
                xcopy(hh, n + 2).start()
                xswap(hh, n).start()
    ring(3)

    for s in range(32):
        @pl.when(p != s)
        def _():
            dcp(0, 0, s).wait_recv()
            dcol[pl.ds(SRC * s, SRC), :] = rcv[s]

        @pl.when(p == s)
        def _():
            dcol[pl.ds(SRC * s, SRC), :] = snd[s]

    def split(rows, t, slot):
        hi = t.astype(BF16)
        rhs[slot, rows, 0:128] = hi
        rhs[slot, rows, 128:256] = (t - hi.astype(F32)).astype(BF16)

    @pl.loop(0, 4)
    def _(i):
        rows = pl.ds(pl.multiple_of(BLK * i, 16), BLK)
        split(rows, dcol[rows, :] * rden[rows, :], 0)

    ring(4)
    for hh in range(2):
        @pl.when(h == hh)
        def _():
            for n in range(2, 4):
                xcopy(hh, n).wait_recv()
                xswap(hh, n).start()
            for dz in range(8):
                zswap(1 - hh, dz).wait_recv()
            for n in range(4):
                xswap(1 - hh, n).wait_recv()
    for rel in range(1, 4):
        conv(rel)

    def block(rel, slot):
        prod = jnp.dot(whi[rel], rhs[slot], preferred_element_type=F32)
        prod = prod[:, 0:128] + prod[:, 128:256]
        prod = prod + jnp.dot(wlo[rel], rhs[slot, :, 0:128], preferred_element_type=F32)
        rows = pl.ds(pl.multiple_of(BLK * lax.rem(x + rel, 4), 16), BLK)
        return rows, (prod + dcol[rows, :]) * rden[rows, :]

    @pl.loop(0, 4)
    def _(rel):
        rows, t = block(rel, 0)
        split(rows, t, 1)

    def c1(n):
        return rcopy(t2.at[n], r1.at[n], c1s.at[n], c1r.at[n], at(p, za, lax.rem(x + 8 - za - n, 4)))

    def c1_own(n):
        return pltpu.make_async_copy(t2.at[n], r1.at[n], c1r.at[n])

    @pl.loop(0, 4)
    def _(n):
        rel = lax.rem(8 - za - n, 4)
        _rows, t = block(rel, 1)
        t2[n] = t

        @pl.when(rel != 0)
        def _():
            c1(n).start()

        @pl.when(rel == 0)
        def _():
            c1_own(n).start()

    pl.semaphore_wait(vsem, 3)

    def mcp(n, j, zb):
        return rcopy(
            msend.at[n * 16 + j], mrecv.at[za * 16 + k], ms.at[n * 16 + j], mr.at[za * 16 + k],
            at(h * 16 + j, zb, x),
        )

    def ucp(n):
        return rcopy(
            tn.at[n, :, pl.ds(pl.multiple_of(64 * (1 - h), 8), 64), :], up.at[n, h],
            us.at[n], ur.at[n], other,
        )

    lane16 = lax.broadcasted_iota(jnp.int32, (16, 128), 1)

    @pl.loop(0, 4)
    def _(n):
        rel = lax.rem(8 - za - n, 4)

        @pl.when(rel != 0)
        def _():
            c1(n).wait_recv()

        @pl.when(rel == 0)
        def _():
            c1_own(n).wait()

        zb = lax.rem(x + za + n, 4)
        for q in range(4):
            if q < 3:
                v = r1[n, pl.ds(128 * q, 128), :]
            else:
                v = jnp.concatenate([r1[n, pl.ds(384, 16), :], jnp.zeros((112, 128), F32)], axis=0)
            tn[n, q] = v.T
        up[n, h] = tn[n, :, pl.ds(pl.multiple_of(64 * h, 8), 64), :]
        ucp(n).start()
        for q in range(3):
            for b in range(2):
                for a in range(4):
                    qs[q, pl.ds(b * 4 + a, 16, stride=8), :] = tn[n, q, pl.ds(a * 32 + b, 16, stride=2), :]
        rest = jnp.zeros((16, 128), F32)
        for b in range(2):
            for a in range(4):
                g = b * 4 + a
                v = tn[n, 3, pl.ds(a * 32 + b, 16, stride=2), :]
                rest = jnp.where(lane16 // 16 == g, v if g == 0 else pltpu.roll(v, 16 * g, 1), rest)
        for j in range(16):
            m = n * 16 + j
            for q in range(3):
                msend[m, 8 * q : 8 * q + 8, :] = qs[q, 8 * j : 8 * j + 8, :]
            msend[m, 24:25, :] = rest[j : j + 1, :]

        @pl.loop(0, 16)
        def _(i):
            j = lax.rem(k + i, 16)
            own = jnp.logical_and(zb == za, h * 16 + j == p)

            @pl.when(jnp.logical_not(own))
            def _():
                mcp(n, j, zb).start()

            @pl.when(own)
            def _():
                mrecv[za * 16 + k] = msend[n * 16 + j]

    @pl.loop(0, 4)
    def _(n):
        ucp(n).wait_recv()

    @pl.loop(0, 64)
    def _(i):
        own = jnp.logical_and(i // 16 == za, 2 * lax.rem(i, 16) + zl == p)

        @pl.when(jnp.logical_not(own))
        def _():
            rcopy(msend.at[0], mrecv.at[i], ms.at[0], mr.at[i], at(p, za, x)).wait_recv()

    sub = lax.broadcasted_iota(jnp.int32, (16, 8, 128), 1) < 4
    for lt in range(2):
        for q in range(4):
            if q < 3:
                v = mrecv[pl.ds(32 * lt, 32), 8 * q : 8 * q + 8, :].reshape(16, 2, 8, 128)
                even, odd = v[:, 0], v[:, 1]
                mirror = (
                    jnp.where(sub, even, pltpu.roll(odd, 4, 1)).reshape(128, 128),
                    jnp.where(sub, pltpu.roll(even, 4, 1), odd).reshape(128, 128),
                )
            else:
                v = mrecv[pl.ds(32 * lt, 32), 24, :]
                for b in range(2):
                    for a in range(4):
                        g = b * 4 + a
                        qs[b, pl.ds(a, 32, stride=4), :] = v if g == 0 else pltpu.roll(v, 128 - 16 * g, 1)
                mirror = (qs[0], qs[1])
            for b in range(2):
                parts = []
                for s in range(4):
                    xs_ = 2 * lt + s // 2
                    n = lax.rem(xs_ + 8 - x - za, 4)
                    parts.append(up[n, s % 2, q, pl.ds(32 * b, 32), :])
                v = (2.0 * jnp.concatenate(parts, axis=0) - mirror[b]).T
                if q < 3:
                    out[pl.ds(512 * q + 2 * lt + b, 128, stride=4), :] = v
                else:
                    out[pl.ds(1536 + 2 * lt + b, 16, stride=4), :] = v[0:16, :]

    for hh in range(2):
        @pl.when(h == hh)
        def _():
            for i in range(1, 4):
                wx(hh, i).wait_send()
            for n in range(4):
                xcopy(hh, n).wait_send()
                xswap(hh, n).wait_send()
            for d in range(ups[hh]):
                zcopy(hh, True, d).wait_send()
            for d in range(downs[hh]):
                zcopy(hh, False, d).wait_send()
            for dz in range(8):
                zswap(hh, dz).wait_send()

    @pl.loop(0, 32)
    def _(i):
        d = 2 * lax.rem(k + i // 2, 16) + lax.rem(i, 2)

        @pl.when(d != p)
        def _():
            dcp(i, d, p).wait_send()

    @pl.loop(0, 4)
    def _(n):
        @pl.when(lax.rem(8 - za - n, 4) != 0)
        def _():
            c1(n).wait_send()

        ucp(n).wait_send()
        zb = lax.rem(x + za + n, 4)

        @pl.loop(0, 16)
        def _(j):
            @pl.when(jnp.logical_not(jnp.logical_and(zb == za, h * 16 + j == p)))
            def _():
                mcp(n, j, zb).wait_send()


def on_device(driver, coupling, eps_occ, eps_vir):
    dma = pltpu.SemaphoreType.DMA
    any_ = pl.BlockSpec(memory_space=pl.ANY)
    smem = pl.BlockSpec(memory_space=pltpu.SMEM)
    vmem = pl.BlockSpec(memory_space=pltpu.VMEM)
    res = pl.pallas_call(
        kernel,
        out_shape=jax.ShapeDtypeStruct((PAIRS, 128), F32),
        in_specs=[any_, any_, smem, smem, vmem],
        out_specs=vmem,
        scratch_shapes=[
            pltpu.VMEM((3200, 64), F32),
            pltpu.VMEM((32, SRC, 128), F32),
            pltpu.VMEM((32, SRC, 128), F32),
            pltpu.VMEM((4, BLK, PAIRS), F32),
            pltpu.VMEM((4, BLK, PAIRS), BF16),
            pltpu.VMEM((4, BLK, PAIRS), BF16),
            pltpu.VMEM((PAIRS, 128), F32),
            pltpu.VMEM((PAIRS, 128), F32),
            pltpu.VMEM((2, PAIRS, 256), BF16),
            pltpu.VMEM((NOCC, 128), F32),
            pltpu.VMEM((4, BLK, 128), F32),
            pltpu.VMEM((4, BLK, 128), F32),
            pltpu.VMEM((4, 4, 128, 128), F32),
            pltpu.VMEM((64, 25, 128), F32),
            pltpu.VMEM((64, 25, 128), F32),
            pltpu.VMEM((4, 2, 4, 64, 128), F32),
            pltpu.VMEM((3, 128, 128), F32),
            dma((2,)),
            pltpu.SemaphoreType.REGULAR,
            dma((3,)), dma((3,)),
            dma((4,)), dma((4,)),
            dma((8,)), dma((8,)),
            dma((12,)), dma((12,)),
            dma((32,)), dma((32,)),
            dma((4,)), dma((4,)),
            dma((64,)), dma((64,)),
            dma((4,)), dma((4,)),
        ],
        compiler_params=pltpu.CompilerParams(
            collective_id=0, has_side_effects=True, vmem_limit_bytes=56 << 20
        ),
    )(driver.reshape(3200, 64), coupling, eps_occ, eps_vir, eps_vir.reshape(2, 128))
    return res.reshape(BLK, 2, 2, 128).transpose(0, 2, 1, 3).reshape(BLK, 2, 256)


def solution(mesh):
    return jax.shard_map(
        on_device,
        mesh=mesh,
        in_specs=(P("pair", "va", "vb"), P("vb", None), P(), P()),
        out_specs=P("vb", ("va", "pair"), None),
        check_vma=False,
    )
```

time: 411 us -> 112 us (0.27)
  blocking collectives: 205 us -> 0 us
  waiting for transfers between devices: 122 us -> 0 us
  Pallas kernels: 0 us -> 109 us
  local copies, waits for them, and re-layouts: 36.3 us -> 2.32 us
  starting transfers between devices: 14.7 us -> 0 us
  between operations: 13.5 us -> 0.01 us
  matrix products: 13.4 us -> 0 us
  other arithmetic: 4.21 us -> 0 us
    all_to_all x8 -> x0, blocking collectives: 205 us -> none  [the longest x2 68.9 us: on_device(): lax.all_to_all(widened, 'pair', split_axis=0, concat_axis=1, tiled=True)]
    pallas_call x0 -> x1, Pallas kernels: none -> 109 us  [on_device(): pl.pallas_call(kernel, out_shape=jax.ShapeDtypeStruct((PAIRS, 128), F32),...]
    all_gather x2 -> x0, waiting for transfers between devices: 96.5 us -> none  [on_device(): lax.all_gather(moved, 'vb', axis=1, tiled=True)]
    all_to_all x1 -> x0, waiting for transfers between devices: 25.1 us -> none  [on_device(): lax.all_to_all(outgoing, ('pair', 'va'), split_axis=1, concat_axis=1, til...]
    all_to_all x10 -> x0, local copies, waits for them, and re-layouts: 17.1 us -> none  [the longest x2 4.97 us: on_device(): lax.all_to_all(outgoing, ('pair', 'va'), split_axis=1, concat_axis=1, til...]
    all_to_all x1 -> x0, starting transfers between devices: 14.6 us -> none  [on_device(): lax.all_to_all(outgoing, ('pair', 'va'), split_axis=1, concat_axis=1, til...]
    dot_general x2 -> x0, matrix products: 13.4 us -> none  [apply_ladder(): jnp.dot(matrix, right, precision=lax.Precision.HIGHEST, preferred_element...]
    reshape x4 -> x0, local copies, waits for them, and re-layouts: 8.74 us -> none  [the longest x2 4.79 us: on_device(): received.reshape(iblock, npair, nva, rchunk, rchunk)]
  transfers between devices with their start and end apart: 3 -> 0, of which waited for: 3 -> 0; matrix products, arithmetic and copies ran while one was open for 1% -> 0% of each run, Pallas kernels for 0% -> 0%
where the time goes in v1:
time: 112 us; the launch traced here: 111 us
  Pallas kernels  109 us (97%)
  local copies, waits for them, and re-layouts  2.32 us (2%)
    pallas_call x1, Pallas kernels, on_device(): pl.pallas_call(kernel, out_shape=jax.ShapeDtypeStruct((PAIRS, 128), F32),...  109 us
    unnamed x1, local copies, waits for them, and re-layouts  2.32 us

profile of v1, /device:TPU:1, one launch (start us, length us, event | category | flops | bytes accessed | tf_op | source)
XLA Modules:
  0.0 111.2 jit_solution(12695330748232288064)
XLA Ops:
  0.0 108.8 %shard_map.46 = f32[1600,128]{1,0:T(8,128)} custom-call(f32[3200,64]{1,0:T(8,128)} %bitcast.8, f32[400,1600]{1,0:T(8,128)} %cpl.1, f32[40]{0:T(128)} %eo.1, f32[256]{0:T(256)} %evs.1, f32[2,128]{1,0:T(2,128)} %bitcast.9), custom_call_target="tpu_custom_call" | custom-call | tf_op jit(solution)/shard_map/pallas_call | solution.py:421
  108.9 2.3 %copy.7 = f32[400,2,256]{2,1,0:T(2,128)} copy(f32[400,2,256]{2,1,0:T(2,128)} %bitcast.7) | data formatting | bytes 1638400

commit v2 on v1

--- a/solution.py
+++ b/solution.py
@@ -91,8 +91,6 @@
         return pl.ds(pl.multiple_of(ZOFF[hh] + ZROWS[hh] * zz, 8), ZROWS[hh])
 
     def xslice(hh, half):
-        if half is None:
-            return pl.ds(XOFF[hh], XROWS[hh])
         return pl.ds(XOFF[hh], XHALF[hh]) if half == 0 else pl.ds(XOFF[hh] + XHALF[hh], XROWS[hh] - XHALF[hh])
 
     def wx(hh, i):
@@ -101,46 +99,52 @@
             at(p, za, lax.rem(x + i, 4)),
         )
 
+    XPIECES = ((0, 3, 0, True), (0, 1, 1, False), (0, 3, 1, True), (0, 1, 0, False), (3, 2, 0, True), (1, 2, 1, False))
+
     def xcopy(hh, n):
-        right, left = at(p, za, lax.rem(x + 1, 4)), at(p, za, lax.rem(x + 3, 4))
-        if n == 0:
-            src, dst, dev = wf.at[0, xslice(hh, None), :], wf.at[3, xslice(hh, None), :], right
-        elif n == 1:
-            src, dst, dev = wf.at[0, xslice(hh, None), :], wf.at[1, xslice(hh, None), :], left
-        elif n == 2:
-            src, dst, dev = wf.at[3, xslice(hh, 0), :], wf.at[2, xslice(hh, 0), :], right
-        else:
-            src, dst, dev = wf.at[1, xslice(hh, 1), :], wf.at[2, xslice(hh, 1), :], left
-        return rcopy(src, dst, xs.at[n], xr.at[n], dev)
+        here, there, half, right = XPIECES[n]
+        return rcopy(
+            wf.at[here, xslice(hh, half), :], wf.at[there, xslice(hh, half), :], xs.at[n], xr.at[n],
+            at(p, za, lax.rem(x + (1 if right else 3), 4)),
+        )
 
     def xswap(hh, n):
-        rel, half = ((3, None), (1, None), (2, 0), (2, 1))[n]
-        ref = wf.at[rel, xslice(hh, half), :]
-        return rcopy(ref, ref, cs.at[8 + n], cr.at[8 + n], other)
-
-    def zcopy(hh, up, d):
-        src = wf.at[pl.ds(1, 3), zslice(hh, lax.rem(z + 8 + (-d if up else d), 8)), :]
-        n = d if up else 4 + d
+        _here, there, half, _right = XPIECES[n]
+        ref = wf.at[there, xslice(hh, half), :]
+        return rcopy(ref, ref, cs.at[24 + n], cr.at[24 + n], other)
+
+    def zpiece(hh, rel, dz):
+        return wf.at[rel, zslice(hh, lax.rem(z + 8 + dz, 8)), :]
+
+    def zcopy(hh, rel, up, d):
+        src = zpiece(hh, rel, -d if up else d)
+        n = 3 * (d if up else 4 + d) + rel - 1
         return rcopy(src, src, zs.at[n], zr.at[n], zdev(1 if up else -1))
 
-    def zwait(hh, up, d):
-        dst = wf.at[pl.ds(1, 3), zslice(hh, lax.rem(z + 8 + (-d if up else d), 8)), :]
-        n = d - 1 if up else 4 + d - 1
+    def zwait(hh, rel, up, d):
+        dst = zpiece(hh, rel, -d if up else d)
+        n = 3 * (d - 1 if up else 4 + d - 1) + rel - 1
         return rcopy(dst, dst, zs.at[n], zr.at[n], zdev(1 if up else -1))
 
-    def zswap(hh, dz):
-        ref = wf.at[pl.ds(1, 3), zslice(hh, lax.rem(z + dz, 8)), :]
-        return rcopy(ref, ref, cs.at[dz], cr.at[dz], other)
+    def zswap(hh, rel, dz):
+        ref = zpiece(hh, rel, dz)
+        n = 3 * dz + rel - 1
+        return rcopy(ref, ref, cs.at[n], cr.at[n], other)
 
     ups, downs = (4, 3), (3, 4)
 
-    for hh in range(2):
-        @pl.when(h == hh)
-        def _():
-            for i in (2, 1, 3):
-                wx(hh, i).start()
-            for n in range(2):
-                xcopy(hh, n).start()
+    def by_core(f):
+        for hh in range(2):
+            @pl.when(h == hh)
+            def _():
+                f(hh)
+
+    @by_core
+    def _(hh):
+        for i in (2, 1, 3):
+            wx(hh, i).start()
+        for n in range(4):
+            xcopy(hh, n).start()
 
     def dcp(i, d, src):
         return rcopy(snd.at[d], rcv.at[src], ds.at[i], dr.at[src], at(d, za, x))
@@ -166,39 +170,44 @@
             whi[rel, rows, :] = hi
             wlo[rel, rows, :] = (v - hi.astype(F32)).astype(BF16)
 
+    RELS = (1, 3, 2)
+
     def ring(d):
-        for hh in range(2):
-            @pl.when(h == hh)
-            def _():
+        @by_core
+        def _(hh):
+            for rel in RELS:
                 if d == 0:
-                    for i in range(1, 4):
-                        wx(hh, i).wait_recv()
-                    zcopy(hh, True, 0).start()
-                    zcopy(hh, False, 0).start()
-                    zswap(hh, 0).start()
-                else:
-                    if d <= ups[hh]:
-                        zwait(hh, True, d).wait_recv()
-                        if d < ups[hh]:
-                            zcopy(hh, True, d).start()
-                        zswap(hh, 8 - d).start()
-                    if d <= downs[hh]:
-                        zwait(hh, False, d).wait_recv()
-                        if d < downs[hh]:
-                            zcopy(hh, False, d).start()
-                        zswap(hh, d).start()
+                    wx(hh, 4 - rel).wait_recv()
+                    zcopy(hh, rel, True, 0).start()
+                    zcopy(hh, rel, False, 0).start()
+                    zswap(hh, rel, 0).start()
+                    continue
+                if d <= ups[hh]:
+                    zwait(hh, rel, True, d).wait_recv()
+                    if d < ups[hh]:
+                        zcopy(hh, rel, True, d).start()
+                    zswap(hh, rel, 8 - d).start()
+                if d <= downs[hh]:
+                    zwait(hh, rel, False, d).wait_recv()
+                    if d < downs[hh]:
+                        zcopy(hh, rel, False, d).start()
+                    zswap(hh, rel, d).start()
+
+    def xstep(first, on):
+        @by_core
+        def _(hh):
+            for n in (first, first + 1):
+                xcopy(hh, n).wait_recv()
+                if on:
+                    xcopy(hh, n + 4).start()
+                xswap(hh, n).start()
 
     ring(0)
     conv(0)
     ring(1)
+    xstep(0, True)
     ring(2)
-    for hh in range(2):
-        @pl.when(h == hh)
-        def _():
-            for n in range(2):
-                xcopy(hh, n).wait_recv()
-                xcopy(hh, n + 2).start()
-                xswap(hh, n).start()
+    xstep(2, False)
     ring(3)
 
     for s in range(32):
@@ -220,20 +229,6 @@
     def _(i):
         rows = pl.ds(pl.multiple_of(BLK * i, 16), BLK)
         split(rows, dcol[rows, :] * rden[rows, :], 0)
-
-    ring(4)
-    for hh in range(2):
-        @pl.when(h == hh)
-        def _():
-            for n in range(2, 4):
-                xcopy(hh, n).wait_recv()
-                xswap(hh, n).start()
-            for dz in range(8):
-                zswap(1 - hh, dz).wait_recv()
-            for n in range(4):
-                xswap(1 - hh, n).wait_recv()
-    for rel in range(1, 4):
-        conv(rel)
 
     def block(rel, slot):
         prod = jnp.dot(whi[rel], rhs[slot], preferred_element_type=F32)
@@ -242,10 +237,23 @@
         rows = pl.ds(pl.multiple_of(BLK * lax.rem(x + rel, 4), 16), BLK)
         return rows, (prod + dcol[rows, :]) * rden[rows, :]
 
-    @pl.loop(0, 4)
-    def _(rel):
+    def first(rel):
         rows, t = block(rel, 0)
         split(rows, t, 1)
+
+    ring(4)
+    xstep(4, False)
+    first(0)
+    for rel in RELS:
+        @by_core
+        def _(hh):
+            for dz in range(8):
+                zswap(1 - hh, rel, dz).wait_recv()
+            for n in range(6):
+                if XPIECES[n][1] == rel:
+                    xswap(1 - hh, n).wait_recv()
+        conv(rel)
+        first(rel)
 
     def c1(n):
         return rcopy(t2.at[n], r1.at[n], c1s.at[n], c1r.at[n], at(p, za, lax.rem(x + 8 - za - n, 4)))
@@ -337,57 +345,56 @@
     def _(n):
         ucp(n).wait_recv()
 
-    @pl.loop(0, 64)
-    def _(i):
-        own = jnp.logical_and(i // 16 == za, 2 * lax.rem(i, 16) + zl == p)
-
-        @pl.when(jnp.logical_not(own))
-        def _():
-            rcopy(msend.at[0], mrecv.at[i], ms.at[0], mr.at[i], at(p, za, x)).wait_recv()
-
-    sub = lax.broadcasted_iota(jnp.int32, (16, 8, 128), 1) < 4
-    for lt in range(2):
+    sub = lax.broadcasted_iota(jnp.int32, (8, 8, 128), 1) < 4
+
+    @pl.loop(0, 4)
+    def _(n):
+        zs_ = lax.rem(za + 8 - x - n, 4)
+
+        @pl.loop(0, 16)
+        def _(j):
+            i = zs_ * 16 + j
+            own = jnp.logical_and(zs_ == za, 2 * j + zl == p)
+
+            @pl.when(jnp.logical_not(own))
+            def _():
+                rcopy(msend.at[0], mrecv.at[i], ms.at[0], mr.at[i], at(p, za, x)).wait_recv()
+
+        m = lax.rem(zs_ + 8 - x - za, 4)
+        rows = pl.ds(pl.multiple_of(64 * zs_, 64), 64)
         for q in range(4):
             if q < 3:
-                v = mrecv[pl.ds(32 * lt, 32), 8 * q : 8 * q + 8, :].reshape(16, 2, 8, 128)
+                v = mrecv[pl.ds(16 * zs_, 16), 8 * q : 8 * q + 8, :].reshape(8, 2, 8, 128)
                 even, odd = v[:, 0], v[:, 1]
                 mirror = (
-                    jnp.where(sub, even, pltpu.roll(odd, 4, 1)).reshape(128, 128),
-                    jnp.where(sub, pltpu.roll(even, 4, 1), odd).reshape(128, 128),
+                    jnp.where(sub, even, pltpu.roll(odd, 4, 1)).reshape(64, 128),
+                    jnp.where(sub, pltpu.roll(even, 4, 1), odd).reshape(64, 128),
                 )
             else:
-                v = mrecv[pl.ds(32 * lt, 32), 24, :]
+                v = mrecv[pl.ds(16 * zs_, 16), 24, :]
                 for b in range(2):
                     for a in range(4):
                         g = b * 4 + a
-                        qs[b, pl.ds(a, 32, stride=4), :] = v if g == 0 else pltpu.roll(v, 128 - 16 * g, 1)
-                mirror = (qs[0], qs[1])
+                        qs[b, pl.ds(a, 16, stride=4), :] = v if g == 0 else pltpu.roll(v, 128 - 16 * g, 1)
+                mirror = (qs[0, 0:64, :], qs[1, 0:64, :])
             for b in range(2):
-                parts = []
-                for s in range(4):
-                    xs_ = 2 * lt + s // 2
-                    n = lax.rem(xs_ + 8 - x - za, 4)
-                    parts.append(up[n, s % 2, q, pl.ds(32 * b, 32), :])
-                v = (2.0 * jnp.concatenate(parts, axis=0) - mirror[b]).T
-                if q < 3:
-                    out[pl.ds(512 * q + 2 * lt + b, 128, stride=4), :] = v
-                else:
-                    out[pl.ds(1536 + 2 * lt + b, 16, stride=4), :] = v[0:16, :]
-
-    for hh in range(2):
-        @pl.when(h == hh)
-        def _():
-            for i in range(1, 4):
-                wx(hh, i).wait_send()
-            for n in range(4):
-                xcopy(hh, n).wait_send()
-                xswap(hh, n).wait_send()
+                mine = jnp.concatenate([up[m, s, q, pl.ds(32 * b, 32), :] for s in range(2)], axis=0)
+                out[q, b, rows, :] = 2.0 * mine - mirror[b]
+
+    @by_core
+    def _(hh):
+        for i in range(1, 4):
+            wx(hh, i).wait_send()
+        for n in range(6):
+            xcopy(hh, n).wait_send()
+            xswap(hh, n).wait_send()
+        for rel in RELS:
             for d in range(ups[hh]):
-                zcopy(hh, True, d).wait_send()
+                zcopy(hh, rel, True, d).wait_send()
             for d in range(downs[hh]):
-                zcopy(hh, False, d).wait_send()
+                zcopy(hh, rel, False, d).wait_send()
             for dz in range(8):
-                zswap(hh, dz).wait_send()
+                zswap(hh, rel, dz).wait_send()
 
     @pl.loop(0, 32)
     def _(i):
@@ -411,6 +418,12 @@
             @pl.when(jnp.logical_not(jnp.logical_and(zb == za, h * 16 + j == p)))
             def _():
                 mcp(n, j, zb).wait_send()
+
+
+def turn(v, out):
+    for lt in range(2):
+        for b in range(2):
+            out[pl.ds(2 * lt + b, 128, stride=4), :] = v[0, b, 128 * lt : 128 * lt + 128, :].T
 
 
 def on_device(driver, coupling, eps_occ, eps_vir):
@@ -420,7 +433,7 @@
     vmem = pl.BlockSpec(memory_space=pltpu.VMEM)
     res = pl.pallas_call(
         kernel,
-        out_shape=jax.ShapeDtypeStruct((PAIRS, 128), F32),
+        out_shape=jax.ShapeDtypeStruct((4, 2, 256, 128), F32),
         in_specs=[any_, any_, smem, smem, vmem],
         out_specs=vmem,
         scratch_shapes=[
@@ -444,9 +457,9 @@
             dma((2,)),
             pltpu.SemaphoreType.REGULAR,
             dma((3,)), dma((3,)),
-            dma((4,)), dma((4,)),
-            dma((8,)), dma((8,)),
-            dma((12,)), dma((12,)),
+            dma((6,)), dma((6,)),
+            dma((24,)), dma((24,)),
+            dma((30,)), dma((30,)),
             dma((32,)), dma((32,)),
             dma((4,)), dma((4,)),
             dma((64,)), dma((64,)),
@@ -456,6 +469,13 @@
             collective_id=0, has_side_effects=True, vmem_limit_bytes=56 << 20
         ),
     )(driver.reshape(3200, 64), coupling, eps_occ, eps_vir, eps_vir.reshape(2, 128))
+    res = pl.pallas_call(
+        turn,
+        grid=(4,),
+        out_shape=jax.ShapeDtypeStruct((PAIRS, 128), F32),
+        in_specs=[pl.BlockSpec((1, 2, 256, 128), lambda i: (i, 0, 0, 0))],
+        out_specs=pl.BlockSpec((512, 128), lambda i: (i, 0)),
+    )(res)
     return res.reshape(BLK, 2, 2, 128).transpose(0, 2, 1, 3).reshape(BLK, 2, 256)
 
 

time: 112 us -> 98.1 us (0.88)
  Pallas kernels: 109 us -> 96.5 us
  local copies, waits for them, and re-layouts: 2.32 us -> 0 us
    pallas_call x1 -> x2, Pallas kernels: 109 us -> 96.5 us  [the longest x1 93 us: on_device(): pl.pallas_call(kernel, out_shape=jax.ShapeDtypeStruct((4, 2, 256, 128), F...]
    unnamed x1 -> x0, local copies, waits for them, and re-layouts: 2.32 us -> none
where the time goes in v2:
time: 98.1 us; the launch traced here: 96.5 us
  Pallas kernels  96.5 us (98%)
    pallas_call x1, Pallas kernels, on_device(): pl.pallas_call(kernel, out_shape=jax.ShapeDtypeStruct((4, 2, 256, 128), F...  93 us
    pallas_call x1, Pallas kernels, on_device(): pl.pallas_call(turn, grid=(4,), out_shape=jax.ShapeDtypeStruct((PAIRS, 12...  3.51 us

profile of v2, /device:TPU:1, one launch (start us, length us, event | category | flops | bytes accessed | tf_op | source)
XLA Modules:
  0.0 96.5 jit_solution(7669970321094866395)
XLA Ops:
  0.0 93.0 %shard_map.46.v = f32[4,2,256,128]{3,2,1,0:T(8,128)} custom-call(f32[3200,64]{1,0:T(8,128)} %bitcast.7, f32[400,1600]{1,0:T(8,128)} %cpl.1, f32[40]{0:T(128)} %eo.1, f32[256]{0:T(256)} %evs.1, f32[2,128]{1,0:T(2,128)} %bitcast.8), custom_call_target="tpu_custom_call" | custom-call | tf_op jit(solution)/shard_map/pallas_call | solution.py:434
  93.0 3.5 %shard_map.47 = f32[1600,128]{1,0:T(8,128)} custom-call(f32[4,2,256,128]{3,2,1,0:T(8,128)} %shard_map.46.v), custom_call_target="tpu_custom_call" | custom-call | tf_op jit(solution)/shard_map/pallas_call | solution.py:472

commit v3 on v2

--- a/solution.py
+++ b/solution.py
@@ -149,17 +149,18 @@
     def dcp(i, d, src):
         return rcopy(snd.at[d], rcv.at[src], ds.at[i], dr.at[src], at(d, za, x))
 
-    @pl.loop(0, 16)
-    def _(i):
-        kk = lax.rem(k + i, 16)
-        rows = [din[pl.ds(4 * kk + a, SRC, stride=64), :] for a in range(4)]
-        for hh in range(2):
-            d = 2 * kk + hh
-            snd[d] = jnp.concatenate([r[:, 32 * hh : 32 * hh + 32] for r in rows], axis=1)
-
-            @pl.when(d != p)
-            def _():
-                dcp(2 * i + hh, d, p).start()
+    def dsend(lo, hi):
+        @pl.loop(lo, hi)
+        def _(i):
+            kk = lax.rem(k + i, 16)
+            rows = [din[pl.ds(4 * kk + a, SRC, stride=64), :] for a in range(4)]
+            for hh in range(2):
+                d = 2 * kk + hh
+                snd[d] = jnp.concatenate([r[:, 32 * hh : 32 * hh + 32] for r in rows], axis=1)
+
+                @pl.when(d != p)
+                def _():
+                    dcp(2 * i + hh, d, p).start()
 
     def conv(rel):
         @pl.loop(0, 5)
@@ -202,6 +203,7 @@
                     xcopy(hh, n + 4).start()
                 xswap(hh, n).start()
 
+    dsend(0, 16)
     ring(0)
     conv(0)
     ring(1)
@@ -255,15 +257,20 @@
         conv(rel)
         first(rel)
 
+    sg = 1 - 2 * lax.rem(y, 2)
+
+    def shift(n):
+        return lax.rem(sg * (za + n) + 8, 4)
+
     def c1(n):
-        return rcopy(t2.at[n], r1.at[n], c1s.at[n], c1r.at[n], at(p, za, lax.rem(x + 8 - za - n, 4)))
+        return rcopy(t2.at[n], r1.at[n], c1s.at[n], c1r.at[n], at(p, za, lax.rem(x + 4 - shift(n), 4)))
 
     def c1_own(n):
         return pltpu.make_async_copy(t2.at[n], r1.at[n], c1r.at[n])
 
     @pl.loop(0, 4)
     def _(n):
-        rel = lax.rem(8 - za - n, 4)
+        rel = lax.rem(4 - shift(n), 4)
         _rows, t = block(rel, 1)
         t2[n] = t
 
@@ -293,7 +300,7 @@
 
     @pl.loop(0, 4)
     def _(n):
-        rel = lax.rem(8 - za - n, 4)
+        rel = lax.rem(4 - shift(n), 4)
 
         @pl.when(rel != 0)
         def _():
@@ -303,7 +310,7 @@
         def _():
             c1_own(n).wait()
 
-        zb = lax.rem(x + za + n, 4)
+        zb = lax.rem(x + shift(n), 4)
         for q in range(4):
             if q < 3:
                 v = r1[n, pl.ds(128 * q, 128), :]
@@ -360,7 +367,7 @@
             def _():
                 rcopy(msend.at[0], mrecv.at[i], ms.at[0], mr.at[i], at(p, za, x)).wait_recv()
 
-        m = lax.rem(zs_ + 8 - x - za, 4)
+        m = lax.rem(sg * (zs_ - x) + 12 - za, 4)
         rows = pl.ds(pl.multiple_of(64 * zs_, 64), 64)
         for q in range(4):
             if q < 3:
@@ -406,12 +413,12 @@
 
     @pl.loop(0, 4)
     def _(n):
-        @pl.when(lax.rem(8 - za - n, 4) != 0)
+        @pl.when(lax.rem(4 - shift(n), 4) != 0)
         def _():
             c1(n).wait_send()
 
         ucp(n).wait_send()
-        zb = lax.rem(x + za + n, 4)
+        zb = lax.rem(x + shift(n), 4)
 
         @pl.loop(0, 16)
         def _(j):
@@ -421,9 +428,11 @@
 
 
 def turn(v, out):
-    for lt in range(2):
-        for b in range(2):
-            out[pl.ds(2 * lt + b, 128, stride=4), :] = v[0, b, 128 * lt : 128 * lt + 128, :].T
+    for q in range(4):
+        n = 128 if q < 3 else 16
+        for lt in range(2):
+            for b in range(2):
+                out[pl.ds(512 * q + 2 * lt + b, n, stride=4), :] = v[q, b, 128 * lt : 128 * lt + 128, :].T[0:n]
 
 
 def on_device(driver, coupling, eps_occ, eps_vir):
@@ -471,10 +480,10 @@
     )(driver.reshape(3200, 64), coupling, eps_occ, eps_vir, eps_vir.reshape(2, 128))
     res = pl.pallas_call(
         turn,
-        grid=(4,),
         out_shape=jax.ShapeDtypeStruct((PAIRS, 128), F32),
-        in_specs=[pl.BlockSpec((1, 2, 256, 128), lambda i: (i, 0, 0, 0))],
-        out_specs=pl.BlockSpec((512, 128), lambda i: (i, 0)),
+        in_specs=[vmem],
+        out_specs=vmem,
+        compiler_params=pltpu.CompilerParams(vmem_limit_bytes=8 << 20),
     )(res)
     return res.reshape(BLK, 2, 2, 128).transpose(0, 2, 1, 3).reshape(BLK, 2, 256)
 

time: 98.1 us -> 94.7 us (0.965); the launches traced: 96.5 us -> 94.5 us
  Pallas kernels: 96.5 us -> 93.3 us
  local copies, waits for them, and re-layouts: 0 us -> 1.22 us
    pallas_call x1, Pallas kernels: 3.51 us -> 1.2 us  [on_device(): pl.pallas_call(turn, out_shape=jax.ShapeDtypeStruct((PAIRS, 128), F32), i...]
    unnamed x0 -> x2, local copies, waits for them, and re-layouts: none -> 1.22 us
where the time goes in v3:
time: 94.7 us; the launch traced here: 94.5 us
  Pallas kernels  93.3 us (99%)
  local copies, waits for them, and re-layouts  1.22 us (1%)
    pallas_call x1, Pallas kernels, on_device(): pl.pallas_call(kernel, out_shape=jax.ShapeDtypeStruct((4, 2, 256, 128), F...  92.1 us

profile of v3, /device:TPU:1, one launch (start us, length us, event | category | flops | bytes accessed | tf_op | source)
XLA Modules:
  0.0 94.5 jit_solution(16920546402802561685)
XLA Ops:
  0.0 92.1 %shard_map.46.v = f32[4,2,256,128]{3,2,1,0:T(8,128)} custom-call(f32[3200,64]{1,0:T(8,128)} %bitcast.7, f32[400,1600]{1,0:T(8,128)} %cpl.1, f32[40]{0:T(128)} %eo.1, f32[256]{0:T(256)} %evs.1, f32[2,128]{1,0:T(2,128)} %bitcast.8), custom_call_target="tpu_custom_call" | custom-call | tf_op jit(solution)/shard_map/pallas_call | solution.py:443
  92.1 0.0 copy-start
  92.1 1.2 %copy-done = f32[4,2,256,128]{3,2,1,0:T(8,128)S(1)} copy-done((f32[4,2,256,128]{3,2,1,0:T(8,128)S(1)}, f32[4,2,256,128]{3,2,1,0:T(8,128)}, u32[]{:S(2)}) %copy-start) | copy-done | bytes 1048600
  93.3 1.2 %shard_map.47 = f32[1600,128]{1,0:T(8,128)} custom-call(f32[4,2,256,128]{3,2,1,0:T(8,128)S(1)} %copy-done), custom_call_target="tpu_custom_call" | custom-call | tf_op jit(solution)/shard_map/pallas_call | solution.py:481
Async XLA Ops:
  92.1 1.2 %copy-start = (f32[4,2,256,128]{3,2,1,0:T(8,128)S(1)}, f32[4,2,256,128]{3,2,1,0:T(8,128)}, u32[]{:S(2)}) copy-start(f32[4,2,256,128]{3,2,1,0:T(8,128)} %shard_map.46.v) | copy-start | bytes 3145732

commit v4 on v3

--- a/solution.py
+++ b/solution.py
@@ -212,6 +212,9 @@
     xstep(2, False)
     ring(3)
 
+    ring(4)
+    xstep(4, False)
+
     for s in range(32):
         @pl.when(p != s)
         def _():
@@ -243,8 +246,6 @@
         rows, t = block(rel, 0)
         split(rows, t, 1)
 
-    ring(4)
-    xstep(4, False)
     first(0)
     for rel in RELS:
         @by_core

time: 94.7 us -> 94.6 us (level)
  no operation moved by 1% of the time
where the time goes in v4:
time: 94.6 us; the launch traced here: 94.4 us
  Pallas kernels  93.2 us (99%)
  local copies, waits for them, and re-layouts  1.22 us (1%)
    pallas_call x1, Pallas kernels, on_device(): pl.pallas_call(kernel, out_shape=jax.ShapeDtypeStruct((4, 2, 256, 128), F...  92 us

profile of v4, /device:TPU:1, one launch (start us, length us, event | category | flops | bytes accessed | tf_op | source)
XLA Modules:
  0.0 94.4 jit_solution(16513880983857657836)
XLA Ops:
  0.0 92.0 %shard_map.46.v = f32[4,2,256,128]{3,2,1,0:T(8,128)} custom-call(f32[3200,64]{1,0:T(8,128)} %bitcast.7, f32[400,1600]{1,0:T(8,128)} %cpl.1, f32[40]{0:T(128)} %eo.1, f32[256]{0:T(256)} %evs.1, f32[2,128]{1,0:T(2,128)} %bitcast.8), custom_call_target="tpu_custom_call" | custom-call | tf_op jit(solution)/shard_map/pallas_call | solution.py:444
  92.0 0.0 copy-start
  92.0 1.2 %copy-done = f32[4,2,256,128]{3,2,1,0:T(8,128)S(1)} copy-done((f32[4,2,256,128]{3,2,1,0:T(8,128)S(1)}, f32[4,2,256,128]{3,2,1,0:T(8,128)}, u32[]{:S(2)}) %copy-start) | copy-done | bytes 1048600
  93.2 1.2 %shard_map.47 = f32[1600,128]{1,0:T(8,128)} custom-call(f32[4,2,256,128]{3,2,1,0:T(8,128)S(1)} %copy-done), custom_call_target="tpu_custom_call" | custom-call | tf_op jit(solution)/shard_map/pallas_call | solution.py:482
Async XLA Ops:
  92.0 1.2 %copy-start = (f32[4,2,256,128]{3,2,1,0:T(8,128)S(1)}, f32[4,2,256,128]{3,2,1,0:T(8,128)}, u32[]{:S(2)}) copy-start(f32[4,2,256,128]{3,2,1,0:T(8,128)} %shard_map.46.v) | copy-start | bytes 3145732
